TPU v7x, 256 devices: a whole 4x4x8 slice. The times are simulated.
256 devices in a mesh: dp: 4 (over x), expert: 8 (over z), etp: 8 (over y, core).
Axes of the slice: x: 4, y: 4, z: 8, core: 2. Of those that a mesh axis runs over, the one named last changes fastest.
Arguments:
- grad_output: bfloat16 [2048, 6144], P(('dp', 'expert', 'etp')), may hold values from -6 to 6
- comb_weights: bfloat16 [2048, 4], P(('dp', 'expert', 'etp')), may hold values from 0.099609375 to 1
- expert_ids: int32 [2048, 4], P(('dp', 'expert', 'etp')), may hold values from 0 to 7, all different within a row; in each aligned block of 8 rows (0 to 7, 8 to 15, ...) at most 6 rows name the same one
- down_weight: bfloat16 [8, 6144, 6144], P('expert', 'etp', 'dp'), may hold values from -0.078125 to 0.078125
- gate_weight: bfloat16 [8, 6144, 6144], P('expert', 'dp', 'etp'), may hold values from -0.078125 to 0.078125
- up_weight: bfloat16 [8, 6144, 6144], P('expert', 'dp', 'etp'), may hold values from -0.078125 to 0.078125
- gate_saved: bfloat16 [8, 1536, 6144], P('expert', None, 'etp'), may hold values from -6 to 6
- up_saved: bfloat16 [8, 1536, 6144], P('expert', None, 'etp'), may hold values from -6 to 6
Outputs:
- input_grad: bfloat16 [2048, 6144], P(('dp', 'expert', 'etp'))
Inputs may be any that keep to these rules, and one draw needn't show every extreme that they name: `expert_ids`: each token names 4 different experts; no expert is named by more than 6 of the tokens of one device.
All inputs are finite; a program needn't handle non-finite values.
Results may differ from a plain program's by a relative error of at most 0.0049.
Values may be sent and summed in bfloat16 or wider, within the bound.
A program may use at most 128 MiB of HBM per device.

v0:
```python
import jax
import jax.numpy as jnp
from jax import lax
from jax.sharding import PartitionSpec as P


def swiglu_backward(hidden_raw, weight, gate_pre, up_pre):
    gate_value = gate_pre.astype(jnp.float32)
    up_value = up_pre.astype(jnp.float32)
    sigmoid_gate = jax.nn.sigmoid(gate_value)
    scaled = hidden_raw * weight[:, None]
    gate_grad = (
        scaled * up_value * sigmoid_gate * (1.0 + gate_value * (1.0 - sigmoid_gate))
    ).astype(jnp.bfloat16)
    up_grad = (scaled * gate_value * sigmoid_gate).astype(jnp.bfloat16)
    return (gate_grad, up_grad)


def on_device(
    grad_output, comb_weights, expert_ids, down_weight, gate_weight, up_weight, gate_saved, up_saved
):
    group_count = lax.axis_size("dp")
    expert_count = lax.axis_size("expert")
    tensor_count = lax.axis_size("etp")
    tokens_here, model_width = grad_output.shape
    choices_count = expert_ids.shape[1]
    capacity = min(
        tokens_here, tokens_here * choices_count // expert_count + max(2, tokens_here // 6)
    )
    quarter = model_width // group_count
    labels = jnp.arange(expert_count, dtype=jnp.int32)
    matches = (expert_ids[:, :, None] == labels[None, None, :]).astype(jnp.int32)
    expert_hits = jnp.sum(matches, axis=1)
    before = jnp.cumsum(expert_hits, axis=0) - expert_hits
    position = jnp.sum(matches * before[:, None, :], axis=2)
    target = expert_ids * capacity + position
    slot_labels = jnp.arange(expert_count * capacity, dtype=jnp.int32)
    chosen = slot_labels[:, None, None] == target[None, :, :]
    selector = (
        jnp.any(chosen, axis=2).astype(jnp.bfloat16).reshape(expert_count, capacity, tokens_here)
    )
    pieces = grad_output.reshape(tokens_here, group_count, quarter)
    outgoing = jnp.einsum(
        "ect,tqd->eqcd", selector, pieces, preferred_element_type=jnp.float32
    ).astype(jnp.bfloat16)
    weight_slots = jnp.sum(
        jnp.where(chosen, comb_weights.astype(jnp.float32)[None, :, :], 0.0), axis=(1, 2)
    )
    weight_out = jnp.broadcast_to(
        weight_slots.reshape(expert_count, 1, capacity), (expert_count, group_count, capacity)
    ).astype(jnp.bfloat16)
    arrived, arrived_weight = (
        lax.all_to_all(outgoing, "dp", split_axis=1, concat_axis=1, tiled=True),
        lax.all_to_all(weight_out, "dp", split_axis=1, concat_axis=1, tiled=True),
    )
    copied = jnp.broadcast_to(
        arrived[:, None], (expert_count, tensor_count, group_count, capacity, quarter)
    )
    copied = copied.reshape(expert_count * tensor_count, group_count, capacity, quarter)
    copied_weight = jnp.broadcast_to(
        arrived_weight[:, None], (expert_count, tensor_count, group_count, capacity)
    )
    copied_weight = copied_weight.reshape(expert_count * tensor_count, group_count, capacity)
    routed, routed_weight = (
        lax.all_to_all(copied, ("expert", "etp"), split_axis=0, concat_axis=0, tiled=True),
        lax.all_to_all(copied_weight, ("expert", "etp"), split_axis=0, concat_axis=0, tiled=True),
    )
    slot_total = expert_count * tensor_count * group_count * capacity
    routed = routed.reshape(slot_total, quarter)
    slot_weight = routed_weight.reshape(slot_total).astype(jnp.float32)
    down_local = down_weight[0]
    gate_local = gate_saved[0]
    up_local = up_saved[0]
    partial_value = jnp.einsum("sq,fq->sf", routed, down_local, preferred_element_type=jnp.float32)
    hidden_raw = lax.psum(partial_value, "dp")
    gate_grad, up_grad = swiglu_backward(hidden_raw, slot_weight, gate_local, up_local)
    slot_grad = jnp.einsum(
        "sf,qf->sq", gate_grad, gate_weight[0], preferred_element_type=jnp.float32
    )
    slot_grad = slot_grad + jnp.einsum(
        "sf,qf->sq", up_grad, up_weight[0], preferred_element_type=jnp.float32
    )
    outbound = slot_grad.reshape(expert_count * tensor_count, group_count, capacity, quarter)
    inbound = lax.all_to_all(outbound, ("expert", "etp"), split_axis=0, concat_axis=0, tiled=True)
    inbound = jnp.sum(
        inbound.reshape(expert_count, tensor_count, group_count, capacity, quarter), axis=1
    )
    complete = lax.all_to_all(inbound, "dp", split_axis=1, concat_axis=3, tiled=True)
    complete = complete.reshape(expert_count * capacity, model_width)
    picked = jnp.take(complete, target.reshape(-1), axis=0)
    picked = picked.reshape(tokens_here, choices_count, model_width)
    return jnp.sum(picked, axis=1).astype(jnp.bfloat16)


def solution(mesh):
    in_specs = (
        P(("dp", "expert", "etp"), None),
        P(("dp", "expert", "etp"), None),
        P(("dp", "expert", "etp"), None),
        P("expert", "etp", "dp"),
        P("expert", "dp", "etp"),
        P("expert", "dp", "etp"),
        P("expert", None, "etp"),
        P("expert", None, "etp"),
    )
    out_specs = P(("dp", "expert", "etp"), None)
    return jax.shard_map(
        on_device, mesh=mesh, in_specs=in_specs, out_specs=out_specs, check_vma=False
    )
```

profile of v0, /device:TPU:32, one launch (start us, length us, event | category | flops | bytes accessed | tf_op | source)
XLA Modules:
  0.0 574.1 jit_solution(5975261550007912184)
XLA Ops:
  6.5 0.0 copy-start
  6.5 0.0 all-reduce.2.cloned.1.call-start
  6.5 0.9 convert_reduce_fusion
  7.5 0.9 select_reduce_fusion.2
  8.4 0.7 compare_and_fusion
  9.1 0.1 fusion.22
  9.2 0.1 reshape.97
  9.2 0.1 copy.61
  9.4 1.2 fusion.9
  10.6 14.3 %all_to_all.40 = bf16[8,4,6,1536]{3,0,2,1:T(8,128)(2,1)S(1)} all-to-all(bf16[8,4,6,1536]{3,0,2,1:T(8,128)(2,1)S(1)} %copy.52), channel_id=1, replica_groups=mesh['dp'=4,'expert'=8,'etp'=8] {'dp'}, dimensions={1} | all-to-all | bytes 1179648 | tf_op jit(solution)/shard_map/all_to_all | solution.py:53
  24.9 0.5 copy.53
  25.4 1.4 broadcast_in_dim.26
  26.8 118.2 %all_to_all.41 = bf16[64,4,6,1536]{3,1,2,0:T(4,128)(2,1)S(1)} all-to-all(bf16[64,4,6,1536]{3,1,2,0:T(4,128)(2,1)S(1)} %bitcast.46), channel_id=1, replica_groups=mesh['dp'=4,'expert'=8,'etp'=8] {'expert','etp'}, dimensions={0} | all-to-all | bytes 9437184 | tf_op jit(solution)/shard_map/all_to_all | solution.py:65
  145.0 4.4 copy.54
  149.4 8.5 %reshape.100 = bf16[1536,1536]{1,0:T(8,128)(2,1)} reshape(bf16[64,4,6,1536]{3,2,1,0:T(8,128)(2,1)} %copy.54) | data formatting | bytes 9437184 | tf_op jit(solution)/shard_map/reshape | solution.py:69
  157.9 9.2 %fusion.16 = f32[1536,768]{1,0:T(8,128)} fusion(bf16[1536,1536]{1,0:T(8,128)(2,1)} %reshape.100, bf16[1,768,1536]{2,1,0:T(8,128)(2,1)} %param.11), kind=kOutput, calls=%fused_computation.22 | convolution fusion | flops 3623878656 | bytes 11796480 | tf_op jit(solution)/shard_map/sq,fq->sf/dot_general | solution.py:74
  167.0 0.0 copy-start.2
  167.0 0.0 all-reduce.2.cloned.1.call-update
  167.1 0.7 copy-done.2
  167.7 0.1 select_reduce_fusion.1
  167.8 0.1 convert_element_type.56
  167.9 7.6 %all_to_all.42 = bf16[8,4,6]{2,0,1:T(8,128)(2,1)S(1)} all-to-all(bf16[8,4,6]{2,0,1:T(8,128)(2,1)S(1)} %broadcast_in_dim.50), channel_id=1, replica_groups=mesh['dp'=4,'expert'=8,'etp'=8] {'dp'}, dimensions={1} | all-to-all | bytes 768 | tf_op jit(solution)/shard_map/all_to_all | solution.py:54
  175.6 15.6 %all_to_all.43 = bf16[64,4,6]{2,1,0:T(4,128)(2,1)S(1)} all-to-all(bf16[64,4,6]{2,1,0:T(4,128)(2,1)S(1)} %bitcast.49), channel_id=1, replica_groups=mesh['dp'=4,'expert'=8,'etp'=8] {'expert','etp'}, dimensions={0} | all-to-all | bytes 6144 | tf_op jit(solution)/shard_map/all_to_all | solution.py:66
  191.2 0.1 reshape.106
  191.4 78.0 %all-reduce.2.cloned.1.call-done = f32[1536,768]{1,0:T(8,128)} async-done(((f32[1536,768]{1,0:T(8,128)}), f32[1536,768]{1,0:T(8,128)}) %all-reduce.2.cloned.1.call-update) | async-done | bytes 4718608 | tf_op jit(solution)/shard_map/psum | solution.py:75
  269.3 0.0 copy-done
  269.3 0.0 copy-start.3
  269.3 0.0 copy-start.4
  269.3 0.0 copy-start.5
  269.4 12.6 %fusion.12 = f32[1536,1536]{1,0:T(8,128)} fusion(bf16[1,1536,768]{2,1,0:T(8,128)(2,1)S(1)} %copy-done, f32[1536,768]{1,0:T(8,128)} %all-reduce.2.cloned.1.call-done, bf16[1,1536,768]{2,1,0:T(8,128)(2,1)} %param.15, bf16[1,1536,768]{2,1,0:T(8,128)(2,1)} %param.14, f32[1536]{0:T(1024)S(1)} %reshape.106), kind=kOutput, calls=%fused_computation.19 | convolution fusion | flops 3639214080 | bytes 21239808 | tf_op jit(solution)/shard_map/sf,qf->sq/dot_general | solution.py:77
  281.9 0.0 copy-done.3
  281.9 0.0 copy-done.4
  281.9 0.0 copy-done.5
  281.9 9.5 %convolution_add_fusion = f32[1536,1536]{1,0:T(8,128)} fusion(f32[1536,1536]{1,0:T(8,128)} %fusion.12, f32[1536,768]{1,0:T(8,128)S(1)} %copy-done.3, bf16[1,1536,768]{2,1,0:T(8,128)(2,1)S(1)} %copy-done.5, bf16[1,1536,768]{2,1,0:T(8,128)(2,1)S(1)} %copy-done.4, f32[1536]{0:T(1024)S(1)} %reshape.106), kind=kOutput, calls=%fused_computation.2 | convolution fusion | flops 3635675136 | bytes 28317696 | tf_op jit(solution)/shard_map/sf,qf->sq/dot_general | solution.py:80
  291.4 11.4 %reshape.102 = f32[64,4,6,1536]{3,2,1,0:T(8,128)} reshape(f32[1536,1536]{1,0:T(8,128)} %convolution_add_fusion) | data formatting | bytes 18874368 | tf_op jit(solution)/shard_map/reshape | solution.py:83
  302.8 17.0 %copy.56 = f32[64,4,6,1536]{3,1,2,0:T(4,128)} copy(f32[64,4,6,1536]{3,2,1,0:T(8,128)} %reshape.102) | data formatting | bytes 18874368 | tf_op jit(solution)/shard_map/reshape | solution.py:83
  319.8 218.2 %all_to_all.44 = f32[64,4,6,1536]{3,1,2,0:T(4,128)S(1)} all-to-all(f32[64,4,6,1536]{3,1,2,0:T(4,128)} %copy.56), channel_id=1, replica_groups=mesh['dp'=4,'expert'=8,'etp'=8] {'expert','etp'}, dimensions={0} | all-to-all | bytes 18874368 | tf_op jit(solution)/shard_map/all_to_all | solution.py:84
  537.9 1.5 bitcast_reduce_fusion
  539.4 1.7 copy.58
  541.1 3.5 all-to-all-start.5
  544.7 0.1 copy.60
  544.8 0.1 reshape.105
  544.8 0.1 copy.50
  544.9 16.9 %all-to-all-done.5 = f32[8,4,6,1536]{3,0,2,1:T(8,128)S(1)} async-done(((f32[8,4,6,1536]{3,0,2,1:T(8,128)}), f32[8,4,6,1536]{3,0,2,1:T(8,128)S(1)}, u32[]{:S(2)}, u32[]{:S(2)}) %all-to-all-start.5) | async-done | bytes 1179680 | tf_op jit(solution)/shard_map/all_to_all | solution.py:88
  561.8 0.8 copy.59
  562.6 0.4 copy.66
  563.0 0.0 copy-start.1
  563.0 1.7 gather_fusion
  564.6 1.4 gather.7
  566.0 1.2 select_reduce_fusion
  567.2 0.0 copy-done.1
  (9 shorter events, 0.1 us)
Async XLA Ops:
  6.5 262.8 %copy-start = (bf16[1,1536,768]{2,1,0:T(8,128)(2,1)S(1)}, bf16[1,1536,768]{2,1,0:T(8,128)(2,1)}, u32[]{:S(2)}) copy-start(bf16[1,1536,768]{2,1,0:T(8,128)(2,1)} %param.12) | copy-start | bytes 7077892
  6.5 262.8 %all-reduce.2.cloned.1.call-start = ((), (), s32[]{:S(2)}) async-start(), calls=%async_computation.6 | async-start | bytes 9437184 | tf_op jit(solution)/shard_map/psum | solution.py:75
  167.0 0.7 copy-start.2
  269.3 12.6 %copy-start.3 = (f32[1536,768]{1,0:T(8,128)S(1)}, f32[1536,768]{1,0:T(8,128)}, u32[]{:S(2)}) copy-start(f32[1536,768]{1,0:T(8,128)} %all-reduce.2.cloned.1.call-done) | copy-start | bytes 14155780
  269.3 12.6 %copy-start.4 = (bf16[1,1536,768]{2,1,0:T(8,128)(2,1)S(1)}, bf16[1,1536,768]{2,1,0:T(8,128)(2,1)}, u32[]{:S(2)}) copy-start(bf16[1,1536,768]{2,1,0:T(8,128)(2,1)} %param.14) | copy-start | bytes 7077892
  269.3 12.6 %copy-start.5 = (bf16[1,1536,768]{2,1,0:T(8,128)(2,1)S(1)}, bf16[1,1536,768]{2,1,0:T(8,128)(2,1)}, u32[]{:S(2)}) copy-start(bf16[1,1536,768]{2,1,0:T(8,128)(2,1)} %param.13) | copy-start | bytes 7077892
  541.1 20.7 %all-to-all-start.5 = ((f32[8,4,6,1536]{3,0,2,1:T(8,128)}), f32[8,4,6,1536]{3,0,2,1:T(8,128)S(1)}, u32[]{:S(2)}, u32[]{:S(2)}) async-start(f32[8,4,6,1536]{3,0,2,1:T(8,128)} %copy.58), calls=%async_computation.5 | async-start | bytes 2359296 | tf_op jit(solution)/shard_map/all_to_all | solution.py:88
  563.0 4.3 copy-start.1
Sparse Core Ops, SparseCore 0:
  167.2 102.1 all-reduce.1
where the time goes:
time: 575 us; the launch traced here: 574 us
  blocking collectives  374 us (65%)
  waiting for transfers between devices  94.9 us (17%)
  local copies, waits for them, and re-layouts  50.4 us (9%)
  matrix products  32.4 us (6%)
  between operations  13.5 us (2%)
    all_to_all x1, blocking collectives, on_device(): lax.all_to_all(outbound, ('expert', 'etp'), split_axis=0, concat_axis=0,...  218 us
    all_to_all x1, blocking collectives, on_device(): lax.all_to_all(copied, ('expert', 'etp'), split_axis=0, concat_axis=0, ti...  118 us
    psum x1, waiting for transfers between devices, on_device(): hidden_raw = lax.psum(partial_value, 'dp')  78 us
    reshape x2, local copies, waits for them, and re-layouts, on_device(): slot_grad.reshape(expert_count * tensor_count, group_count, capacity, qua...  28.4 us
    all_to_all x1, waiting for transfers between devices, on_device(): lax.all_to_all(inbound, 'dp', split_axis=1, concat_axis=3, tiled=True)  16.9 us
    all_to_all x1, blocking collectives, on_device(): lax.all_to_all(copied_weight, ('expert', 'etp'), split_axis=0, concat_axi...  15.6 us
    all_to_all x1, blocking collectives, on_device(): lax.all_to_all(outgoing, 'dp', split_axis=1, concat_axis=1, tiled=True)  14.3 us
    dot_general x1, matrix products, on_device(): jnp.einsum('sf,qf->sq', gate_grad, gate_weight[0], preferred_element_type...  12.6 us
  transfers between devices with their start and end apart: 2, of which 2 were waited for; matrix products, arithmetic and copies ran while one was open for 0% of the time, Pallas kernels for 0%

commit v1 on v0

--- a/solution.py
+++ b/solution.py
@@ -72,7 +72,11 @@
     gate_local = gate_saved[0]
     up_local = up_saved[0]
     partial_value = jnp.einsum("sq,fq->sf", routed, down_local, preferred_element_type=jnp.float32)
-    hidden_raw = lax.psum(partial_value, "dp")
+    hidden_raw = partial_value
+    for hop in (1, 2):
+        hidden_raw = hidden_raw + lax.ppermute(
+            hidden_raw, "dp", [(dev, dev ^ hop) for dev in range(4)]
+        )
     gate_grad, up_grad = swiglu_backward(hidden_raw, slot_weight, gate_local, up_local)
     slot_grad = jnp.einsum(
         "sf,qf->sq", gate_grad, gate_weight[0], preferred_element_type=jnp.float32

time: 575 us -> 686 us (1.19)
  blocking collectives: 374 us -> 465 us
  waiting for transfers between devices: 94.9 us -> 120 us
  between operations: 13.5 us -> 0.15 us
    ppermute x0 -> x2, waiting for transfers between devices: none -> 104 us  [on_device(): lax.ppermute(hidden_raw, 'dp', [(dev, dev ^ hop) for dev in range(4)])]
    all_to_all x1, blocking collectives: 7.65 us -> 104 us  [on_device(): lax.all_to_all(weight_out, 'dp', split_axis=1, concat_axis=1, tiled=True)]
    psum x1 -> x0, waiting for transfers between devices: 78 us -> none  [on_device(): hidden_raw = lax.psum(partial_value, 'dp')]
  transfers between devices with their start and end apart: 2 -> 3, of which waited for: 2 -> 2; matrix products, arithmetic and copies ran while one was open for 0% -> 0% of each run, Pallas kernels for 0% -> 0%
where the time goes in v1:
time: 686 us; the launch traced here: 685 us
  blocking collectives  465 us (68%)
  waiting for transfers between devices  120 us (17%)
  local copies, waits for them, and re-layouts  49.8 us (7%)
  matrix products  36.6 us (5%)
  other arithmetic  8.17 us (1%)
    all_to_all x1, blocking collectives, on_device(): lax.all_to_all(outbound, ('expert', 'etp'), split_axis=0, concat_axis=0,...  213 us
    all_to_all x1, blocking collectives, on_device(): lax.all_to_all(copied, ('expert', 'etp'), split_axis=0, concat_axis=0, ti...  118 us
    all_to_all x1, blocking collectives, on_device(): lax.all_to_all(weight_out, 'dp', split_axis=1, concat_axis=1, tiled=True)  104 us
    ppermute x2, waiting for transfers between devices, on_device(): lax.ppermute(hidden_raw, 'dp', [(dev, dev ^ hop) for dev in range(4)])  104 us
    reshape x2, local copies, waits for them, and re-layouts, on_device(): slot_grad.reshape(expert_count * tensor_count, group_count, capacity, qua...  28.4 us
    all_to_all x1, waiting for transfers between devices, on_device(): lax.all_to_all(inbound, 'dp', split_axis=1, concat_axis=3, tiled=True)  16.8 us
    dot_general x1, matrix products, on_device(): jnp.einsum('sf,qf->sq', up_grad, up_weight[0], preferred_element_type=jnp...  14.8 us
    all_to_all x1, blocking collectives, on_device(): lax.all_to_all(copied_weight, ('expert', 'etp'), split_axis=0, concat_axi...  14.6 us
  transfers between devices with their start and end apart: 3, of which 2 were waited for; matrix products, arithmetic and copies ran while one was open for 0% of the time, Pallas kernels for 0%

profile of v1, /device:TPU:32, one launch (start us, length us, event | category | flops | bytes accessed | tf_op | source)
XLA Modules:
  0.0 684.9 jit_solution(17150475184462956700)
XLA Ops:
  0.0 0.0 copy-start
  0.0 0.9 convert_reduce_fusion
  0.9 0.9 select_reduce_fusion.2
  1.8 0.7 compare_and_fusion
  2.5 0.1 fusion.20
  2.6 0.1 reshape.97
  2.7 0.1 copy.61
  2.9 1.2 fusion.9
  4.1 14.3 %all_to_all.40 = bf16[8,4,6,1536]{3,0,2,1:T(8,128)(2,1)S(1)} all-to-all(bf16[8,4,6,1536]{3,0,2,1:T(8,128)(2,1)S(1)} %copy.52), channel_id=1, replica_groups=mesh['dp'=4,'expert'=8,'etp'=8] {'dp'}, dimensions={1} | all-to-all | bytes 1179648 | tf_op jit(solution)/shard_map/all_to_all | solution.py:53
  18.4 0.5 copy.53
  18.8 1.4 broadcast_in_dim.26
  20.2 118.2 %all_to_all.41 = bf16[64,4,6,1536]{3,1,2,0:T(4,128)(2,1)S(1)} all-to-all(bf16[64,4,6,1536]{3,1,2,0:T(4,128)(2,1)S(1)} %bitcast.46), channel_id=1, replica_groups=mesh['dp'=4,'expert'=8,'etp'=8] {'expert','etp'}, dimensions={0} | all-to-all | bytes 9437184 | tf_op jit(solution)/shard_map/all_to_all | solution.py:65
  138.4 4.4 copy.54
  142.9 8.5 %reshape.100 = bf16[1536,1536]{1,0:T(8,128)(2,1)} reshape(bf16[64,4,6,1536]{3,2,1,0:T(8,128)(2,1)} %copy.54) | data formatting | bytes 9437184 | tf_op jit(solution)/shard_map/reshape | solution.py:69
  151.3 6.4 fusion.16
  157.8 0.0 copy-start.2
  157.8 0.6 collective-permute-start
  158.4 103.6 %collective-permute-done = f32[1536,768]{1,0:T(8,128)S(1)} collective-permute-done((f32[1536,768]{1,0:T(8,128)S(1)}, f32[1536,768]{1,0:T(8,128)S(1)}, u32[]{:S(2)}, u32[]{:S(2)}) %collective-permute-start) | collective-permute-done | bytes 4718624 | tf_op jit(solution)/shard_map/ppermute | solution.py:77
  262.0 2.7 add.43
  264.8 1.0 collective-permute-start.1
  265.8 0.0 copy-done.2
  265.8 0.1 select_reduce_fusion.1
  265.9 0.1 convert_element_type.56
  266.0 104.0 %all_to_all.42 = bf16[8,4,6]{2,0,1:T(8,128)(2,1)S(1)} all-to-all(bf16[8,4,6]{2,0,1:T(8,128)(2,1)S(1)} %broadcast_in_dim.50), channel_id=1, replica_groups=mesh['dp'=4,'expert'=8,'etp'=8] {'dp'}, dimensions={1} | all-to-all | bytes 768 | tf_op jit(solution)/shard_map/all_to_all | solution.py:54
  370.0 14.6 %all_to_all.43 = bf16[64,4,6]{2,1,0:T(4,128)(2,1)S(1)} all-to-all(bf16[64,4,6]{2,1,0:T(4,128)(2,1)S(1)} %bitcast.49), channel_id=1, replica_groups=mesh['dp'=4,'expert'=8,'etp'=8] {'expert','etp'}, dimensions={0} | all-to-all | bytes 6144 | tf_op jit(solution)/shard_map/all_to_all | solution.py:66
  384.6 0.1 reshape.106
  384.7 0.0 copy-start.3
  384.8 0.0 copy-start.4
  384.8 0.0 collective-permute-done.1
  384.8 0.0 copy-done
  384.8 14.1 %fusion.12 = f32[1536,1536]{1,0:T(8,128)} fusion(bf16[1,1536,768]{2,1,0:T(8,128)(2,1)S(1)} %copy-done, bf16[1,1536,768]{2,1,0:T(8,128)(2,1)} %param.15, bf16[1,1536,768]{2,1,0:T(8,128)(2,1)} %param.14, f32[1536,768]{1,0:T(8,128)} %add.43, f32[1536,768]{1,0:T(8,128)} %collective-permute-done.1, f32[1536]{0:T(1024)S(1)} %reshape.106), kind=kOutput, calls=%fused_computation.20 | convolution fusion | flops 3640393728 | bytes 25958400 | tf_op jit(solution)/shard_map/sf,qf->sq/dot_general | solution.py:81
  398.9 0.0 copy-done.3
  398.9 0.0 copy-done.4
  398.9 14.8 %convolution_add_fusion = f32[1536,1536]{1,0:T(8,128)} fusion(f32[1536,1536]{1,0:T(8,128)} %fusion.12, bf16[1,1536,768]{2,1,0:T(8,128)(2,1)S(1)} %copy-done.4, bf16[1,1536,768]{2,1,0:T(8,128)(2,1)S(1)} %copy-done.3, f32[1536,768]{1,0:T(8,128)} %add.43, f32[1536,768]{1,0:T(8,128)} %collective-permute-done.1, f32[1536]{0:T(1024)S(1)} %reshape.106), kind=kOutput, calls=%fused_computation.2 | convolution fusion | flops 3636854784 | bytes 33036288 | tf_op jit(solution)/shard_map/sf,qf->sq/dot_general | solution.py:84
  413.7 11.4 %reshape.102 = f32[64,4,6,1536]{3,2,1,0:T(8,128)} reshape(f32[1536,1536]{1,0:T(8,128)} %convolution_add_fusion) | data formatting | bytes 18874368 | tf_op jit(solution)/shard_map/reshape | solution.py:87
  425.1 17.0 %copy.56 = f32[64,4,6,1536]{3,1,2,0:T(4,128)} copy(f32[64,4,6,1536]{3,2,1,0:T(8,128)} %reshape.102) | data formatting | bytes 18874368 | tf_op jit(solution)/shard_map/reshape | solution.py:87
  442.1 213.5 %all_to_all.44 = f32[64,4,6,1536]{3,1,2,0:T(4,128)S(1)} all-to-all(f32[64,4,6,1536]{3,1,2,0:T(4,128)} %copy.56), channel_id=1, replica_groups=mesh['dp'=4,'expert'=8,'etp'=8] {'expert','etp'}, dimensions={0} | all-to-all | bytes 18874368 | tf_op jit(solution)/shard_map/all_to_all | solution.py:88
  655.6 1.5 bitcast_reduce_fusion
  657.1 1.7 copy.58
  658.8 3.5 all-to-all-start.5
  662.3 0.1 copy.60
  662.4 0.1 reshape.105
  662.5 0.1 copy.50
  662.6 16.8 %all-to-all-done.5 = f32[8,4,6,1536]{3,0,2,1:T(8,128)S(1)} async-done(((f32[8,4,6,1536]{3,0,2,1:T(8,128)}), f32[8,4,6,1536]{3,0,2,1:T(8,128)S(1)}, u32[]{:S(2)}, u32[]{:S(2)}) %all-to-all-start.5) | async-done | bytes 1179680 | tf_op jit(solution)/shard_map/all_to_all | solution.py:92
  679.4 0.8 copy.59
  680.2 0.4 copy.66
  680.6 0.0 copy-start.1
  680.6 1.7 gather_fusion
  682.3 1.4 gather.7
  683.6 1.2 select_reduce_fusion
  684.9 0.0 copy-done.1
  (9 shorter events, 0.1 us)
Async XLA Ops:
  0.0 384.8 %copy-start = (bf16[1,1536,768]{2,1,0:T(8,128)(2,1)S(1)}, bf16[1,1536,768]{2,1,0:T(8,128)(2,1)}, u32[]{:S(2)}) copy-start(bf16[1,1536,768]{2,1,0:T(8,128)(2,1)} %param.12) | copy-start | bytes 7077892
  157.8 108.0 %copy-start.2 = (bf16[8,4]{0,1:T(4,128)(2,1)S(1)}, bf16[8,4]{0,1:T(4,128)(2,1)}, u32[]{:S(2)}) copy-start(bf16[8,4]{0,1:T(4,128)(2,1)} %param.9) | copy-start | bytes 196
  157.8 104.2 %collective-permute-start = (f32[1536,768]{1,0:T(8,128)S(1)}, f32[1536,768]{1,0:T(8,128)S(1)}, u32[]{:S(2)}, u32[]{:S(2)}) collective-permute-start(f32[1536,768]{1,0:T(8,128)S(1)} %fusion.16), channel_id=1, source_target_pairs={{0,64},{64,0},{128,192},{192,128},{1,65},{65,1},{129,193},{193,129... | collective-permute-start | bytes 14155784 | tf_op jit(solution)/shard_map/ppermute | solution.py:77
  264.8 120.0 %collective-permute-start.1 = (f32[1536,768]{1,0:T(8,128)}, f32[1536,768]{1,0:T(8,128)}, u32[]{:S(2)}, u32[]{:S(2)}) collective-permute-start(f32[1536,768]{1,0:T(8,128)} %add.43), channel_id=1, source_target_pairs={{0,128},{64,192},{128,0},{192,64},{1,129},{65,193},{129,1},{193,65... | collective-permute-start | bytes 14155784 | tf_op jit(solution)/shard_map/ppermute | solution.py:77
  384.7 14.2 %copy-start.3 = (bf16[1,1536,768]{2,1,0:T(8,128)(2,1)S(1)}, bf16[1,1536,768]{2,1,0:T(8,128)(2,1)}, u32[]{:S(2)}) copy-start(bf16[1,1536,768]{2,1,0:T(8,128)(2,1)} %param.14) | copy-start | bytes 7077892
  384.8 14.2 %copy-start.4 = (bf16[1,1536,768]{2,1,0:T(8,128)(2,1)S(1)}, bf16[1,1536,768]{2,1,0:T(8,128)(2,1)}, u32[]{:S(2)}) copy-start(bf16[1,1536,768]{2,1,0:T(8,128)(2,1)} %param.13) | copy-start | bytes 7077892
  658.8 20.6 %all-to-all-start.5 = ((f32[8,4,6,1536]{3,0,2,1:T(8,128)}), f32[8,4,6,1536]{3,0,2,1:T(8,128)S(1)}, u32[]{:S(2)}, u32[]{:S(2)}) async-start(f32[8,4,6,1536]{3,0,2,1:T(8,128)} %copy.58), calls=%async_computation.5 | async-start | bytes 2359296 | tf_op jit(solution)/shard_map/all_to_all | solution.py:92
  680.6 4.3 copy-start.1
